TPU v7x, 128 devices: a whole 4x4x4 slice. The times are simulated.
128 devices in a mesh: row: 16 (over z, y), col: 8 (over x, core).
Axes of the slice: x: 4, y: 4, z: 4, core: 2. Of those that a mesh axis runs over, the one named last changes fastest.
Arguments:
- frames: bfloat16 [1048576, 1024], P(('row', 'col')), may hold values from -5 to 5
- frame_counts: int32 [128, 64], P(('row', 'col')), may hold values from 0 to 1000, as said below
- slot_ids: int32 [128, 64], P(('row', 'col')), may hold values from 0 to 4096, as said below
- seed_labels: int32 [4096], P(('row', 'col')), may hold values from 0 to 1023
- attn_query: bfloat16 [1024, 8], replicated, may hold values from -0.1875 to 0.1875
- emb_weight: bfloat16 [8192, 256], replicated, may hold values from -0.0625 to 0.0625
- plda_weight: bfloat16 [256, 256], replicated
Outputs:
- label_scores: float32 [4096, 256], P(('row', 'col'))
Inputs may be any that keep to these rules, and one draw needn't show every extreme that they name: `slot_ids`: each utterance 0 to 4095 sits in exactly one slot whose frame count is positive; slots with count 0 hold 4096. Every utterance of owner o has its home block (utterance // 32) in o's grid column, that is with the same index along col as o; among one owner's utterances at most 4 have the same home block; each home block holds 32 utterances. `frame_counts`: an owner's live slots come first, their frames lie back to back from its first frame slot and sum to at most 8192; a live count is 100 or more. In each grid column, the owners of grid rows 4g to 4g + 3 hold 8, 24, 32 and 64 utterances in some order.
All inputs are finite; a program needn't handle non-finite values.
Results may differ from a plain program's by a relative error of at most 0.0034.
Values may be sent and summed in bfloat16 or wider, within the bound.
A program may use at most 64 MiB of HBM per device.

v0:
```python
import jax
import jax.numpy as jnp
from jax import lax
from jax.sharding import PartitionSpec as P

K = 256
FPU = 256
ITERS = 3


GAIN = 4.0
BETA = 8.0
ALPHA = 0.9
EPSILON = 1e-06


def pool_owner(frames, counts, attn_query, emb_weight):
    ends = jnp.cumsum(counts)
    starts = ends - counts
    frame_index = jnp.arange(frames.shape[0], dtype=jnp.int32)
    member = (
        (frame_index[None, :] >= starts[:, None]) & (frame_index[None, :] < ends[:, None])
    ).astype(jnp.float32)
    energy = jnp.exp(
        GAIN * jnp.tanh(jnp.dot(frames, attn_query, preferred_element_type=jnp.float32))
    ).T
    weight_total = jnp.dot(member, energy.T, precision=lax.Precision.HIGHEST)
    weight_total = weight_total + (counts == 0).astype(jnp.float32)[:, None]
    attention = (member[:, None, :] * energy[None, :, :] / weight_total[:, :, None]).astype(
        jnp.bfloat16
    )
    attention = attention.reshape(-1, frames.shape[0])
    pooled = jnp.dot(attention, frames, preferred_element_type=jnp.float32).astype(jnp.bfloat16)
    pooled = pooled.reshape(counts.shape[0], -1)
    return jnp.dot(pooled, emb_weight, preferred_element_type=jnp.float32).astype(jnp.bfloat16)


def unit_rows(values):
    return values / jnp.sqrt(jnp.mean(values * values, axis=1, keepdims=True) + EPSILON)


def on_device(frames, frame_counts, slot_ids, seed_labels, attn_query, emb_weight, plda_weight):
    counts = frame_counts[0]
    idents = slot_ids[0]
    embed = pool_owner(frames, counts, attn_query, emb_weight)
    width = embed.shape[1]
    home_rows = seed_labels.shape[0]
    grid_rows = lax.axis_size("row")
    grid_cols = lax.axis_size("col")
    column_utts = home_rows * grid_rows
    live = counts > 0
    column_index = jnp.where(
        live, idents // home_rows // grid_cols * home_rows + idents % home_rows, column_utts
    )
    padded = (
        jnp.zeros((column_utts, width), jnp.float32)
        .at[column_index]
        .set(embed.astype(jnp.float32), mode="drop")
    )
    padded_len = (
        jnp.zeros((column_utts,), jnp.float32)
        .at[column_index]
        .set(counts.astype(jnp.float32), mode="drop")
    )
    home_sum, home_len = (
        lax.psum_scatter(padded, "row", scatter_dimension=0, tiled=True),
        lax.psum_scatter(padded_len, "row", scatter_dimension=0, tiled=True),
    )
    home_embed = home_sum.astype(jnp.bfloat16)
    row_unit = unit_rows(home_embed.astype(jnp.float32)).astype(jnp.bfloat16)
    projected = jnp.dot(home_embed, plda_weight, preferred_element_type=jnp.float32)
    col_unit = unit_rows(projected).astype(jnp.bfloat16)
    col_weight = home_len / FPU
    row_vecs = lax.all_gather(row_unit, "col", axis=0, tiled=True)
    cosine = (
        jnp.dot(
            row_vecs,
            lax.all_gather(col_unit, "row", axis=0, tiled=True).T,
            preferred_element_type=jnp.float32,
        )
        / width
    )
    fresh = (
        lax.all_gather(col_weight.astype(jnp.bfloat16), "row", axis=0, tiled=True).astype(
            jnp.float32
        )[None, :]
        * jnp.exp(BETA * cosine)
    ).astype(jnp.bfloat16)
    row_part = jnp.sum(fresh.astype(jnp.float32), axis=1)
    seeds = (seed_labels[:, None] == jnp.arange(K, dtype=jnp.int32)[None, :]).astype(jnp.float32)
    labels = seeds
    totals = lax.psum_scatter(row_part, "col", scatter_dimension=0, tiled=True)
    remaining = ITERS
    for step_index in range(remaining):
        spread = lax.psum_scatter(
            jnp.dot(
                fresh,
                lax.all_gather(labels.astype(jnp.bfloat16), "row", axis=0, tiled=True),
                preferred_element_type=jnp.float32,
            ),
            "col",
            scatter_dimension=0,
            tiled=True,
        )
        labels = ALPHA * spread / totals[:, None] + (1.0 - ALPHA) * seeds
    return jnp.log(1.0 + K * labels)


def solution(mesh):
    return jax.shard_map(
        on_device,
        mesh=mesh,
        in_specs=(
            P(("row", "col"), None),
            P(("row", "col"), None),
            P(("row", "col"), None),
            P(("row", "col")),
            P(),
            P(),
            P(),
        ),
        out_specs=P(("row", "col"), None),
        check_vma=False,
    )
```

profile of v0, /device:TPU:1, one launch (start us, length us, event | category | flops | bytes accessed | tf_op | source)
XLA Modules:
  0.0 323.3 jit_solution(5233481792525376027)
XLA Ops:
  6.5 0.0 copy-start
  6.5 0.0 reduce-scatter.5.cloned.1.call-start
  6.5 0.7 compare_convert_fusion
  7.2 0.7 copy.13
  8.0 0.1 reduce-window.7
  8.1 0.1 reduce
  8.2 0.7 bitcast_subtract_fusion
  8.9 0.3 fusion.11
  9.2 10.2 %fusion.2 = f32[8192,8]{0,1:T(8,128)S(1)} fusion(bf16[8192,1024]{1,0:T(8,128)(2,1)} %param.7, bf16[1024,8]{0,1:T(8,128)(2,1)} %param.11), kind=kOutput, calls=%fused_computation.6 | convolution fusion | flops 134283264 | bytes 17055744 | tf_op jit(solution)/shard_map/dot_general | solution.py:25
  19.4 1.4 fusion.19
  20.8 0.1 copy.14
  20.9 0.1 div.93
  21.0 0.0 copy-start.3
  21.0 0.0 copy-start.4
  21.0 12.6 %fusion.12 = bf16[512,1024]{1,0:T(8,128)(2,1)S(1)} fusion(bf16[8192,1024]{1,0:T(8,128)(2,1)} %param.7, f32[512]{0:T(512)S(1)} %div.93, f32[8,8192]{1,0:T(8,128)S(1)} %bitcast.49, f32[64,8192]{1,0:T(8,128)S(1)} %fusion.11), kind=kOutput, calls=%fused_computation.16 | convolution fusion | flops 8603041792 | bytes 20187136 | tf_op jit(solution)/shard_map/dot_general | solution.py:33
  33.6 0.0 copy-start.2
  33.6 0.0 copy-start.1
  33.6 0.5 reshape.265
  34.2 0.0 copy-done.3
  34.2 0.0 copy-done.4
  34.2 0.0 copy-start.5
  34.2 3.0 fusion.18
  37.2 1.6 scatter_custom_fusion.1
  38.8 0.0 reduce-scatter.5.cloned.1.call-update
  38.8 0.0 reduce-scatter.7.cloned.1.call-start
  38.9 0.8 scatter_custom_fusion
  39.7 0.0 copy-done.2
  39.7 0.7 fusion.40
  41.7 35.5 %all-reduce.1 = f32[512]{0:T(512)S(1)} all-reduce(f32[512]{0:T(512)S(1)} %scatter_custom_fusion), channel_id=2, replica_groups=mesh['row'=16,'col'=8] {'row'}, use_global_device_ids=true, to_apply=%region_1.2.clone | all-reduce | flops 512 | bytes 4096
  77.2 0.1 fusion.37
  77.3 0.2 dynamic-update-slice
  77.5 28.5 %all-reduce = bf16[512]{0:T(512)(128)(2,1)S(1)} all-reduce(bf16[512]{0:T(512)(128)(2,1)S(1)} %dynamic-update-slice), channel_id=1, replica_groups=mesh['row'=16,'col'=8] {'row'}, use_global_device_ids=true, to_apply=%add | all-reduce | flops 512 | bytes 2048
  106.0 0.0 copy-done.1
  106.0 0.1 convert_convert_fusion
  106.1 18.2 %all_gather.21 = bf16[512,256]{1,0:T(8,128)(2,1)S(1)} all-gather(bf16[32,256]{1,0:T(8,128)(2,1)S(1)} %convert_convert_fusion), channel_id=1, replica_groups=mesh['row'=16,'col'=8] {'row'}, dimensions={0}, use_global_device_ids=true | all-gather | bytes 278528 | tf_op jit(solution)/shard_map/all_gather | solution.py:98
  124.3 0.0 reduce-scatter.5.cloned.1.call-done
  124.3 0.0 copy-done
  124.3 1.0 multiply_reduce_fusion
  125.4 0.1 divide_convert_fusion
  125.4 16.4 %all_gather.20 = bf16[512,256]{1,0:T(8,128)(2,1)S(1)} all-gather(bf16[32,256]{1,0:T(8,128)(2,1)S(1)} %divide_convert_fusion), channel_id=1, replica_groups=mesh['row'=16,'col'=8] {'row'}, dimensions={0}, use_global_device_ids=true | all-gather | bytes 278528 | tf_op jit(solution)/shard_map/all_gather | solution.py:78
  141.9 0.9 fusion.26
  142.8 0.8 fusion.27
  143.6 38.0 %all_gather.19 = bf16[256,256]{1,0:T(8,128)(2,1)S(1)} all-gather(bf16[32,256]{1,0:T(8,128)(2,1)S(1)} %fusion.27), channel_id=1, replica_groups=mesh['row'=16,'col'=8] {'col'}, dimensions={0}, use_global_device_ids=true | all-gather | bytes 147456 | tf_op jit(solution)/shard_map/all_gather | solution.py:74
  181.6 0.4 convert_reduce_fusion
  182.0 0.9 fusion.41
  182.9 0.0 reduce-scatter.7.cloned.1.call-update
  182.9 0.0 reduce-scatter.9.cloned.1.call-start
  183.0 0.0 copy-done.5
  183.0 0.6 dynamic-slice.3
  184.2 12.0 %all-reduce.2 = f32[256]{0:T(256)S(1)} all-reduce(f32[256]{0:T(256)S(1)} %get-tuple-element.9), channel_id=5, replica_groups=mesh['row'=16,'col'=8] {'col'}, use_global_device_ids=true, to_apply=%region_9.10.clone | all-reduce | flops 256 | bytes 2048
  196.2 0.1 dynamic-slice.4
  196.3 12.7 %reduce-scatter.7.cloned.1.call-done = f32[32,256]{1,0:T(8,128)} async-done(((f32[256,256]{1,0:T(8,128)}), f32[32,256]{1,0:T(8,128)}) %reduce-scatter.7.cloned.1.call-update) | async-done | bytes 32784 | tf_op jit(solution)/shard_map/reduce_scatter | solution.py:95
  209.0 0.8 fusion.28
  209.8 19.0 %all_gather.22 = bf16[512,256]{1,0:T(8,128)(2,1)S(1)} all-gather(bf16[32,256]{1,0:T(8,128)(2,1)S(1)} %fusion.28), channel_id=1, replica_groups=mesh['row'=16,'col'=8] {'row'}, dimensions={0}, use_global_device_ids=true | all-gather | bytes 278528 | tf_op jit(solution)/shard_map/all_gather | solution.py:98
  228.8 0.9 fusion.42
  229.7 0.0 reduce-scatter.9.cloned.1.call-update
  229.7 0.0 reduce-scatter.11.cloned.1.call-start
  229.8 32.3 %reduce-scatter.9.cloned.1.call-done = f32[32,256]{1,0:T(8,128)} async-done(((f32[256,256]{1,0:T(8,128)}), f32[32,256]{1,0:T(8,128)}) %reduce-scatter.9.cloned.1.call-update) | async-done | bytes 32784 | tf_op jit(solution)/shard_map/reduce_scatter | solution.py:95
  262.1 0.8 fusion.29
  263.0 18.9 %all_gather.23 = bf16[512,256]{1,0:T(8,128)(2,1)S(1)} all-gather(bf16[32,256]{1,0:T(8,128)(2,1)S(1)} %fusion.29), channel_id=1, replica_groups=mesh['row'=16,'col'=8] {'row'}, dimensions={0}, use_global_device_ids=true | all-gather | bytes 278528 | tf_op jit(solution)/shard_map/all_gather | solution.py:98
  281.9 0.9 fusion.43
  282.8 0.0 reduce-scatter.11.cloned.1.call-update
  282.8 32.4 %reduce-scatter.11.cloned.1.call-done = f32[32,256]{1,0:T(8,128)} async-done(((f32[256,256]{1,0:T(8,128)}), f32[32,256]{1,0:T(8,128)}) %reduce-scatter.11.cloned.1.call-update) | async-done | bytes 32784 | tf_op jit(solution)/shard_map/reduce_scatter | solution.py:95
  315.3 1.5 fusion.32
  (6 shorter events, 0.1 us)
Async XLA Ops:
  6.5 117.8 %copy-start = (bf16[256,256]{1,0:T(8,128)(2,1)S(1)}, bf16[256,256]{1,0:T(8,128)(2,1)}, u32[]{:S(2)}) copy-start(bf16[256,256]{1,0:T(8,128)(2,1)} %param.13) | copy-start | bytes 393220
  6.5 117.8 %reduce-scatter.5.cloned.1.call-start = ((), (), s32[]{:S(2)}) async-start(), calls=%async_computation.4 | async-start | bytes 557056 | tf_op jit(solution)/shard_map/reduce_scatter | solution.py:66
  21.0 13.2 %copy-start.3 = (s32[1,64]{1,0:T(1,128)S(1)}, s32[1,64]{1,0:T(1,128)}, u32[]{:S(2)}) copy-start(s32[1,64]{1,0:T(1,128)} %param.8) | copy-start | bytes 772
  21.0 13.2 %copy-start.4 = (s32[1,64]{1,0:T(1,128)S(1)}, s32[1,64]{1,0:T(1,128)}, u32[]{:S(2)}) copy-start(s32[1,64]{1,0:T(1,128)} %param.9) | copy-start | bytes 772
  33.6 6.1 %copy-start.2 = (u32[128]{0:T(128)S(1)}, u32[128]{0:T(128)}, u32[]{:S(2)}) copy-start(u32[128]{0:T(128)} %constant.80) | copy-start | bytes 1540
  33.6 72.4 %copy-start.1 = (s32[32]{0:T(128)S(1)}, s32[32]{0:T(128)}, u32[]{:S(2)}) copy-start(s32[32]{0:T(128)} %param.10) | copy-start | bytes 388
  34.2 148.8 %copy-start.5 = (u32[128]{0:T(128)S(1)}, u32[128]{0:T(128)}, u32[]{:S(2)}) copy-start(u32[128]{0:T(128)} %constant.90) | copy-start | bytes 1540
  38.8 170.1 %reduce-scatter.7.cloned.1.call-start = ((), (), s32[]{:S(2)}) async-start(), calls=%async_computation.5 | async-start | bytes 294912 | tf_op jit(solution)/shard_map/reduce_scatter | solution.py:95
  182.9 79.2 %reduce-scatter.9.cloned.1.call-start = ((), (), s32[]{:S(2)}) async-start(), calls=%async_computation.6 | async-start | bytes 294912 | tf_op jit(solution)/shard_map/reduce_scatter | solution.py:95
  229.7 85.5 %reduce-scatter.11.cloned.1.call-start = ((), (), s32[]{:S(2)}) async-start(), calls=%async_computation.7 | async-start | bytes 294912 | tf_op jit(solution)/shard_map/reduce_scatter | solution.py:95
Sparse Core Ops, SparseCore 0:
  39.0 74.0 reduce-scatter.4
  183.1 25.8 reduce-scatter.6
  229.9 32.2 reduce-scatter.8
  283.0 32.2 reduce-scatter.10
where the time goes:
time: 326 us; the launch traced here: 323 us
  blocking collectives  187 us (57%)
  waiting for transfers between devices  77.5 us (24%)
  matrix products  31.3 us (10%)
  between operations  15.3 us (5%)
  other arithmetic  7.03 us (2%)
  local copies, waits for them, and re-layouts  5.36 us (2%)
    reduce_scatter x3, waiting for transfers between devices, on_device(): lax.psum_scatter(jnp.dot(fresh, lax.all_gather(labels.astype(jnp.bfloat16...  77.4 us
    unnamed x3, blocking collectives  76 us
    all_gather x3, blocking collectives, on_device(): lax.all_gather(labels.astype(jnp.bfloat16), 'row', axis=0, tiled=True)  56.1 us
    all_gather x1, blocking collectives, on_device(): row_vecs = lax.all_gather(row_unit, 'col', axis=0, tiled=True)  38 us
    all_gather x1, blocking collectives, on_device(): lax.all_gather(col_unit, 'row', axis=0, tiled=True)  16.4 us
    dot_general x1, matrix products, pool_owner(): jnp.dot(attention, frames, preferred_element_type=jnp.float32)  12.6 us
    dot_general x1, matrix products, pool_owner(): jnp.dot(frames, attn_query, preferred_element_type=jnp.float32)  10.2 us
  transfers between devices with their start and end apart: 4, of which 3 were waited for; matrix products, arithmetic and copies ran while one was open for 1% of the time, Pallas kernels for 0%

commit v1 on v0

v1 whole, which is shorter than its diff:
```python
import functools

import jax
import jax.numpy as jnp
from jax import lax
from jax.experimental import pallas as pl
from jax.experimental.pallas import tpu as pltpu
from jax.sharding import PartitionSpec as P

MESH = pl.DeviceIdType.MESH
F32 = jnp.float32
BF16 = jnp.bfloat16

D = 1024
HEADS = 8
E = 256
K = 256
FPU = 256
SLOTS = 64
HOME = 32
ROWS = 16
COLS = 8
WIN = 1024
WINDOWS = 8
SEG = 16
ITERS = 3

GAIN = 4.0
BETA = 8.0
ALPHA = 0.9
EPSILON = 1e-06

NT = (((1,), (1,)), ((), ()))
TN = (((0,), (0,)), ((), ()))

PACK, ROWU, COLU, META, TOTS, SUMS, LABS = 0, 1, 2, 3, 4, 5, 8
N_SEMS = 10


def iota(shape, dim):
    return lax.broadcasted_iota(jnp.int32, shape, dim)


def to_column(row, size):
    shape = (size, row.shape[1])
    return jnp.sum(jnp.where(iota(shape, 0) == iota(shape, 1), row, 0.0), axis=1, keepdims=True)


def unit_rows(values):
    return values / jnp.sqrt(jnp.mean(values * values, axis=1, keepdims=True) + EPSILON)


def kernel(
    frames, counts, idents, seeds, query, emb_weight, plda, out,
    frame_buf, weight_buf, segments, packed, inbox, row_units, col_units, metas, meta_own,
    affinity, parts, part_send, part_in, tot_send, tot_in, labels_buf,
    frame_sem, weight_sem, send, recv,
):
    r = lax.axis_index("row")
    c = lax.axis_index("col")
    row_peers = [(lax.rem(r + k, ROWS), c) for k in range(1, ROWS)]
    col_peers = [(r, lax.rem(c + k, COLS)) for k in range(1, COLS)]

    barrier = pltpu.get_barrier_semaphore()
    for peer in row_peers + col_peers:
        pl.semaphore_signal(barrier, inc=1, device_id=peer, device_id_type=MESH)

    def frame_copy(w):
        return pltpu.make_async_copy(
            frames.at[pl.ds(w * WIN, WIN)], frame_buf.at[w], frame_sem.at[w]
        )

    for w in range(WINDOWS):
        frame_copy(w).start()
    weight_copy = pltpu.make_async_copy(emb_weight, weight_buf, weight_sem)
    weight_copy.start()

    live_row = counts[...].astype(F32)
    square = (SLOTS, SLOTS)
    count_square = jnp.broadcast_to(live_row, square)
    ends = jnp.sum(
        jnp.where(iota(square, 1) <= iota(square, 0), count_square, 0.0), axis=1, keepdims=True
    )
    count_col = to_column(live_row, SLOTS)
    starts = ends - count_col
    query_t = query[...].astype(F32).T.astype(BF16)

    def window(w, weight_total):
        frame_copy(w).wait()
        block = frame_buf[w]
        score = lax.dot_general(query_t, block, NT, preferred_element_type=F32)
        energy = jnp.exp(GAIN * jnp.tanh(score))
        first = (w * WIN).astype(F32)
        index = first + iota((SLOTS, WIN), 1).astype(F32)
        past = ends <= index
        rel = jnp.sum(jnp.where(past & (ends > first), 1.0, 0.0), axis=0, keepdims=True)
        member = jnp.where((starts <= index) & (ends > index), 1.0, 0.0).astype(BF16)
        mask = rel == iota((SEG, WIN), 0).astype(F32)
        rows = jnp.concatenate(
            [jnp.where(mask, energy[h : h + 1, :], 0.0) for h in range(HEADS)], axis=0
        ).astype(BF16)
        sums = jnp.dot(rows, block, preferred_element_type=F32)
        for h in range(HEADS):
            segments[h, pl.ds(w * SEG, SEG), :] = sums[h * SEG : (h + 1) * SEG].astype(BF16)
        high = energy.astype(BF16).astype(F32)
        both = jnp.concatenate([high, energy - high], axis=0).astype(BF16)
        return weight_total + lax.dot_general(member, both, NT, preferred_element_type=F32)

    weight_total = lax.fori_loop(0, WINDOWS, window, jnp.zeros((SLOTS, 2 * HEADS), F32))

    wide = (SLOTS, WINDOWS * SEG)
    before = jnp.where(ends <= (iota(wide, 1) // SEG * WIN).astype(F32), 1.0, 0.0)
    target = jnp.sum(before, axis=0, keepdims=True) + (iota((1, WINDOWS * SEG), 1) % SEG).astype(F32)
    gather = jnp.where(target == iota(wide, 0).astype(F32), 1.0, 0.0).astype(BF16)
    dead = jnp.where(count_col > 0.0, 0.0, 1.0)
    weight_copy.wait()
    total = jnp.zeros((SLOTS, E), F32)
    for h in range(HEADS):
        pooled = jnp.dot(gather, segments[h], preferred_element_type=F32)
        scale = weight_total[:, h : h + 1] + weight_total[:, HEADS + h : HEADS + h + 1] + dead
        pooled = (pooled / scale).astype(BF16)
        total = total + jnp.dot(
            pooled, weight_buf[h * D : (h + 1) * D, :], preferred_element_type=F32
        )
    embed = total.astype(BF16)

    ident_row = idents[...]
    dest_row = jnp.where(counts[...] > 0, ident_row // (HOME * COLS), ROWS).astype(F32)
    place_row = (ident_row % HOME).astype(F32)
    dest_col = to_column(dest_row, SLOTS)
    place_col = to_column(place_row, SLOTS)
    same = (dest_col == dest_row) & (iota(square, 0) < iota(square, 1))
    rank_row = jnp.sum(jnp.where(same, 1.0, 0.0), axis=0, keepdims=True)
    spot = dest_row * 16.0 + rank_row
    high_col = jnp.floor(count_col * (1.0 / 256.0))
    lane = iota((SLOTS, 128), 1)
    meta = jnp.where(
        lane == 0,
        place_col + 1.0,
        jnp.where(lane == 1, high_col, jnp.where(lane == 2, count_col - 256.0 * high_col, 0.0)),
    ).astype(BF16)
    place = iota((ROWS * 16, SLOTS), 0).astype(F32)
    letter = jnp.zeros((ROWS * 16, 128), F32)
    for t, part in enumerate((embed[:, :128], embed[:, 128:], meta)):
        pick = jnp.where(place == spot + 4.0 * t, 1.0, 0.0).astype(BF16)
        letter = letter + jnp.dot(pick, part, preferred_element_type=F32)
    packed[...] = letter.astype(BF16)

    pl.semaphore_wait(barrier, ROWS + COLS - 2)
    for peer in row_peers:
        pltpu.make_async_remote_copy(
            packed.at[pl.ds(peer[0] * 16, 16)], inbox.at[pl.ds(r * 16, 16)],
            send.at[PACK], recv.at[PACK], device_id=peer, device_id_type=MESH,
        ).start()
    own = pl.multiple_of(r * 16, 16)
    inbox[pl.ds(own, 16), :] = packed[pl.ds(own, 16), :]
    seed_row = jnp.minimum(seeds[...], K).astype(F32)
    seed_col = to_column(seed_row, HOME)
    seed_hot = jnp.where(seed_col == iota((HOME, K), 1).astype(F32), 1.0, 0.0)

    def wait_bytes(ref, sem):
        pltpu.make_async_copy(ref, ref, sem).wait()

    wait_bytes(inbox.at[pl.ds(0, (ROWS - 1) * 16)], recv.at[PACK])

    got = inbox[...]
    mark = jnp.broadcast_to(got[:, 0:1].astype(F32), (ROWS * 16, 128))
    sub = iota((ROWS * 16, 128), 0) % 16
    lane = iota((ROWS * 16, 128), 1)
    mark = jnp.where(
        sub < 4,
        pltpu.roll(mark, ROWS * 16 - 8, 0),
        jnp.where(sub < 8, pltpu.roll(mark, ROWS * 16 - 4, 0), mark),
    )
    pick = (mark == (lane % HOME + 1).astype(F32)) & (lane // HOME == sub // 4) & (sub < 12)
    home = lax.dot_general(
        jnp.where(pick, 1.0, 0.0).astype(BF16), got, TN, preferred_element_type=F32
    )
    home_embed = jnp.concatenate([home[0:HOME], home[HOME : 2 * HOME]], axis=1)
    unit = unit_rows(home_embed).astype(BF16)
    row_own = pl.multiple_of(c * HOME, HOME)
    col_own = pl.multiple_of(r * HOME, HOME)
    row_units[pl.ds(row_own, HOME), :] = unit
    for peer in col_peers:
        pltpu.make_async_remote_copy(
            row_units.at[pl.ds(row_own, HOME)], row_units.at[pl.ds(row_own, HOME)],
            send.at[ROWU], recv.at[ROWU], device_id=peer, device_id_type=MESH,
        ).start()
    projected = jnp.dot(home_embed.astype(BF16), plda[...], preferred_element_type=F32)
    col_units[pl.ds(col_own, HOME), :] = unit_rows(projected).astype(BF16)
    for peer in row_peers:
        pltpu.make_async_remote_copy(
            col_units.at[pl.ds(col_own, HOME)], col_units.at[pl.ds(col_own, HOME)],
            send.at[COLU], recv.at[COLU], device_id=peer, device_id_type=MESH,
        ).start()
    home_meta = home[2 * HOME : 3 * HOME]
    diagonal = iota((HOME, 128), 0) == iota((HOME, 128), 1) % HOME
    group = iota((HOME, 128), 1) // HOME
    values = jnp.where(
        group == 0, home_meta[:, 1:2], jnp.where(group == 1, home_meta[:, 2:3], seed_col)
    )
    meta_own[0] = jnp.sum(jnp.where(diagonal, values, 0.0), axis=0, keepdims=True)
    metas[r] = meta_own[0]
    for peer in row_peers:
        pltpu.make_async_remote_copy(
            meta_own.at[0], metas.at[r],
            send.at[META], recv.at[META], device_id=peer, device_id_type=MESH,
        ).start()

    wait_bytes(metas.at[pl.ds(0, ROWS - 1)], recv.at[META])
    shape = (128, ROWS * HOME)
    spread_lane = iota(shape, 1) % HOME
    spread_sub = iota(shape, 0)
    take_len = jnp.where(spread_sub == spread_lane, 256.0, 0.0) + jnp.where(
        spread_sub == spread_lane + HOME, 1.0, 0.0
    )
    take_seed = jnp.where(spread_sub == spread_lane + 2 * HOME, 1.0, 0.0)
    meta_rows = jnp.concatenate([metas[k] for k in range(ROWS)], axis=0).astype(BF16)
    mine = iota((ROWS, ROWS * HOME), 0) == iota((ROWS, ROWS * HOME), 1) // HOME

    def column_row(take):
        full = jnp.dot(meta_rows, take.astype(BF16), preferred_element_type=F32)
        return jnp.sum(jnp.where(mine, full, 0.0), axis=0, keepdims=True)

    len_row = column_row(take_len) * (1.0 / FPU)
    seeds_row = column_row(take_seed)
    seeds_t = jnp.where(seeds_row == iota((K, ROWS * HOME), 0).astype(F32), 1.0, 0.0).astype(BF16)

    wait_bytes(row_units.at[pl.ds(0, (COLS - 1) * HOME)], recv.at[ROWU])
    wait_bytes(col_units.at[pl.ds(0, (ROWS - 1) * HOME)], recv.at[COLU])
    cosine = lax.dot_general(row_units[...], col_units[...], NT, preferred_element_type=F32)
    affinity[...] = (len_row * jnp.exp(cosine * (BETA / E))).astype(BF16)

    tot_send[0] = lax.dot_general(
        jnp.ones((8, ROWS * HOME), BF16), affinity[...], NT, preferred_element_type=F32
    )[0:1]
    for k, peer in enumerate(col_peers):
        pltpu.make_async_remote_copy(
            tot_send.at[0], tot_in.at[k],
            send.at[TOTS], recv.at[TOTS], device_id=peer, device_id_type=MESH,
        ).start()

    totals = None
    for step in range(ITERS):
        if step == 0:
            part = lax.dot_general(affinity[...], seeds_t, NT, preferred_element_type=F32)
        else:
            wait_bytes(
                labels_buf.at[step - 1, pl.ds(0, (ROWS - 1) * HOME)], recv.at[LABS + step - 1]
            )
            part = jnp.dot(affinity[...], labels_buf[step - 1], preferred_element_type=F32)
        parts[...] = part
        part_send[step] = part.astype(BF16)
        for k, peer in enumerate(col_peers):
            pltpu.make_async_remote_copy(
                part_send.at[step, pl.ds(peer[1] * HOME, HOME)], part_in.at[step, k],
                send.at[SUMS + step], recv.at[SUMS + step], device_id=peer, device_id_type=MESH,
            ).start()
        if step == 0:
            wait_bytes(tot_in, recv.at[TOTS])
            row_totals = tot_send[0]
            for k in range(COLS - 1):
                row_totals = row_totals + tot_in[k]
            here = iota((HOME, COLS * HOME), 1) == iota((HOME, COLS * HOME), 0) + c * HOME
            totals = jnp.sum(jnp.where(here, row_totals, 0.0), axis=1, keepdims=True)
        wait_bytes(part_in.at[step], recv.at[SUMS + step])
        spread = parts[pl.ds(row_own, HOME), :]
        for k in range(COLS - 1):
            spread = spread + part_in[step, k].astype(F32)
        labels = ALPHA * spread / totals + (1.0 - ALPHA) * seed_hot
        if step < ITERS - 1:
            labels_buf[step, pl.ds(col_own, HOME), :] = labels.astype(BF16)
            for peer in row_peers:
                pltpu.make_async_remote_copy(
                    labels_buf.at[step, pl.ds(col_own, HOME)],
                    labels_buf.at[step, pl.ds(col_own, HOME)],
                    send.at[LABS + step], recv.at[LABS + step], device_id=peer, device_id_type=MESH,
                ).start()
        else:
            out[...] = jnp.log(1.0 + K * labels)

    wait_bytes(packed.at[pl.ds(0, (ROWS - 1) * 16)], send.at[PACK])
    wait_bytes(row_units.at[pl.ds(0, (COLS - 1) * HOME)], send.at[ROWU])
    wait_bytes(col_units.at[pl.ds(0, (ROWS - 1) * HOME)], send.at[COLU])
    wait_bytes(metas.at[pl.ds(0, ROWS - 1)], send.at[META])
    wait_bytes(tot_in, send.at[TOTS])
    for step in range(ITERS):
        wait_bytes(part_in.at[step], send.at[SUMS + step])
    for step in range(ITERS - 1):
        wait_bytes(labels_buf.at[step, pl.ds(0, (ROWS - 1) * HOME)], send.at[LABS + step])


def on_device(frames, frame_counts, slot_ids, seed_labels, attn_query, emb_weight, plda_weight):
    vmem = pl.BlockSpec(memory_space=pltpu.VMEM)
    hbm = pl.BlockSpec(memory_space=pl.ANY)
    return pl.pallas_call(
        kernel,
        name="speaker_linking",
        out_shape=jax.ShapeDtypeStruct((HOME, K), F32),
        in_specs=[hbm, vmem, vmem, vmem, vmem, hbm, vmem],
        out_specs=vmem,
        scratch_shapes=[
            pltpu.VMEM((WINDOWS, WIN, D), BF16),
            pltpu.VMEM((HEADS * D, E), BF16),
            pltpu.VMEM((HEADS, WINDOWS * SEG, D), BF16),
            pltpu.VMEM((ROWS * 16, 128), BF16),
            pltpu.VMEM((ROWS * 16, 128), BF16),
            pltpu.VMEM((COLS * HOME, E), BF16),
            pltpu.VMEM((ROWS * HOME, E), BF16),
            pltpu.VMEM((ROWS, 1, 128), F32),
            pltpu.VMEM((1, 1, 128), F32),
            pltpu.VMEM((COLS * HOME, ROWS * HOME), BF16),
            pltpu.VMEM((COLS * HOME, K), F32),
            pltpu.VMEM((ITERS, COLS * HOME, K), BF16),
            pltpu.VMEM((ITERS, COLS - 1, HOME, K), BF16),
            pltpu.VMEM((1, 1, COLS * HOME), F32),
            pltpu.VMEM((COLS - 1, 1, COLS * HOME), F32),
            pltpu.VMEM((ITERS - 1, ROWS * HOME, K), BF16),
            pltpu.SemaphoreType.DMA((WINDOWS,)),
            pltpu.SemaphoreType.DMA,
            pltpu.SemaphoreType.DMA((N_SEMS,)),
            pltpu.SemaphoreType.DMA((N_SEMS,)),
        ],
        compiler_params=pltpu.CompilerParams(
            collective_id=0, has_side_effects=True, vmem_limit_bytes=48 * 1024 * 1024
        ),
    )(
        frames, frame_counts, slot_ids, seed_labels.reshape(1, HOME), attn_query, emb_weight,
        plda_weight,
    )


def solution(mesh):
    return jax.shard_map(
        on_device,
        mesh=mesh,
        in_specs=(
            P(("row", "col"), None),
            P(("row", "col"), None),
            P(("row", "col"), None),
            P(("row", "col")),
            P(),
            P(),
            P(),
        ),
        out_specs=P(("row", "col"), None),
        check_vma=False,
    )
```

time: 326 us -> 61.3 us (0.19)
  blocking collectives: 187 us -> 0 us
  waiting for transfers between devices: 77.5 us -> 0 us
  Pallas kernels: 0 us -> 54.5 us
  matrix products: 31.3 us -> 0 us
  between operations: 15.3 us -> 0.03 us
  other arithmetic: 7.03 us -> 0 us
    all_gather x5 -> x0, blocking collectives: 111 us -> none  [the longest x3 56.1 us: on_device(): lax.all_gather(labels.astype(jnp.bfloat16), 'row', axis=0, tiled=True)]
    reduce_scatter x4 -> x0, waiting for transfers between devices: 77.4 us -> none  [the longest x3 77.4 us: on_device(): lax.psum_scatter(jnp.dot(fresh, lax.all_gather(labels.astype(jnp.bfloat16...]
    unnamed x3 -> x0, blocking collectives: 76 us -> none
    pallas_call x0 -> x1, Pallas kernels: none -> 54.5 us  [on_device(): pl.pallas_call(kernel, name='speaker_linking', out_shape=jax.ShapeDtypeSt...]
    dot_general x9 -> x0, matrix products: 31.3 us -> none  [the longest x1 12.6 us: pool_owner(): jnp.dot(attention, frames, preferred_element_type=jnp.float32)]
    unnamed x17 -> x12, local copies, waits for them, and re-layouts: 1.55 us -> 6.55 us
    convert_element_type x10 -> x0, other arithmetic: 3.79 us -> none  [the longest x3 1.74 us: on_device(): labels.astype(jnp.bfloat16)]
  transfers between devices with their start and end apart: 4 -> 0, of which waited for: 3 -> 0; matrix products, arithmetic and copies ran while one was open for 1% -> 0% of each run, Pallas kernels for 0% -> 0%
where the time goes in v1:
time: 61.3 us; the launch traced here: 61.1 us
  Pallas kernels  54.5 us (89%)
  local copies, waits for them, and re-layouts  6.55 us (11%)
    pallas_call x1, Pallas kernels, on_device(): pl.pallas_call(kernel, name='speaker_linking', out_shape=jax.ShapeDtypeSt...  54.5 us
    unnamed x12, local copies, waits for them, and re-layouts  6.55 us

profile of v1, /device:TPU:1, one launch (start us, length us, event | category | flops | bytes accessed | tf_op | source)
XLA Modules:
  0.0 61.1 jit_solution(7620340286301339734)
XLA Ops:
  0.0 0.9 %copy.8.query = bf16[1024,8]{1,0:T(8,128)(2,1)S(1)} copy(bf16[1024,8]{0,1:T(8,128)(2,1)} %param.11) | data formatting | bytes 32768 | tf_op args[4]
  0.9 0.0 copy-start
  0.9 2.2 %copy-done = bf16[8192,256]{1,0:T(8,128)(2,1)S(1)} copy-done((bf16[8192,256]{1,0:T(8,128)(2,1)S(1)}, bf16[8192,256]{1,0:T(8,128)(2,1)}, u32[]{:S(2)}) %copy-start) | copy-done | bytes 4194328
  3.1 0.0 copy-start.1
  3.1 0.9 %copy-done.1 = bf16[256,256]{1,0:T(8,128)(2,1)S(1)} copy-done((bf16[256,256]{1,0:T(8,128)(2,1)S(1)}, bf16[256,256]{1,0:T(8,128)(2,1)}, u32[]{:S(2)}) %copy-start.1) | copy-done | bytes 131096
  4.0 0.0 copy-start.2
  4.0 0.7 %copy-done.2 = s32[1,64]{1,0:T(1,128)S(1)} copy-done((s32[1,64]{1,0:T(1,128)S(1)}, s32[1,64]{1,0:T(1,128)}, u32[]{:S(2)}) %copy-start.2) | copy-done | bytes 280
  4.6 0.0 copy-start.3
  4.6 0.7 %copy-done.3 = s32[1,64]{1,0:T(1,128)S(1)} copy-done((s32[1,64]{1,0:T(1,128)S(1)}, s32[1,64]{1,0:T(1,128)}, u32[]{:S(2)}) %copy-start.3) | copy-done | bytes 280
  5.3 0.0 copy-start.4
  5.3 0.7 %copy-done.4 = s32[32]{0:T(128)S(1)} copy-done((s32[32]{0:T(128)S(1)}, s32[32]{0:T(128)}, u32[]{:S(2)}) %copy-start.4) | copy-done | bytes 152
  6.0 54.5 %speaker_linking.1 = f32[32,256]{1,0:T(8,128)S(1)} custom-call(bf16[8192,1024]{1,0:T(8,128)(2,1)} %frames.1, s32[1,64]{1,0:T(1,128)S(1)} %copy-done.2, s32[1,64]{1,0:T(1,128)S(1)} %copy-done.3, s32[1,32]{1,0:T(1,128)S(1)} %bitcast.1, bf16[1024,8]{1,0:T(8,128)(2,1)S(1)} %copy.8.query, bf16[8192,256]{1,0:T(8,128)(2,1)S(1)} %copy-done, ...), custom_call_target="tpu_custom_call" | custom-call | tf_op jit(solution)/shard_map/speaker_linking/pallas_call | solution.py:296
  60.4 0.6 %copy.10 = f32[32,256]{1,0:T(8,128)} copy(f32[32,256]{1,0:T(8,128)S(1)} %speaker_linking.1) | data formatting | bytes 65536
Async XLA Ops:
  0.9 2.2 %copy-start = (bf16[8192,256]{1,0:T(8,128)(2,1)S(1)}, bf16[8192,256]{1,0:T(8,128)(2,1)}, u32[]{:S(2)}) copy-start(bf16[8192,256]{1,0:T(8,128)(2,1)} %emb_weight.1) | copy-start | bytes 12582916
  3.1 0.9 %copy-start.1 = (bf16[256,256]{1,0:T(8,128)(2,1)S(1)}, bf16[256,256]{1,0:T(8,128)(2,1)}, u32[]{:S(2)}) copy-start(bf16[256,256]{1,0:T(8,128)(2,1)} %plda.1) | copy-start | bytes 393220
  4.0 0.7 %copy-start.2 = (s32[1,64]{1,0:T(1,128)S(1)}, s32[1,64]{1,0:T(1,128)}, u32[]{:S(2)}) copy-start(s32[1,64]{1,0:T(1,128)} %counts.1) | copy-start | bytes 772
  4.6 0.7 %copy-start.3 = (s32[1,64]{1,0:T(1,128)S(1)}, s32[1,64]{1,0:T(1,128)}, u32[]{:S(2)}) copy-start(s32[1,64]{1,0:T(1,128)} %idents.1) | copy-start | bytes 772
  5.3 0.7 %copy-start.4 = (s32[32]{0:T(128)S(1)}, s32[32]{0:T(128)}, u32[]{:S(2)}) copy-start(s32[32]{0:T(128)} %param.10) | copy-start | bytes 388

commit v2 on v1

v2 whole, which is shorter than its diff:
```python
import jax
import jax.numpy as jnp
from jax import lax
from jax.experimental import pallas as pl
from jax.experimental.pallas import tpu as pltpu
from jax.sharding import PartitionSpec as P

MESH = pl.DeviceIdType.MESH
F32 = jnp.float32
BF16 = jnp.bfloat16

D = 1024
HEADS = 8
E = 256
K = 256
FPU = 256
SLOTS = 64
HOME = 32
ROWS = 16
COLS = 8
WIN = 1024
WINDOWS = 8
SEG = 16
SEGS = WINDOWS * SEG
ITERS = 3

GAIN = 4.0
BETA = 8.0
ALPHA = 0.9
EPSILON = 1e-06

NT = (((1,), (1,)), ((), ()))

EARLY, PACK, ROWU, COLU, META, TOTS, SUMS, LABS = 0, 1, 2, 3, 4, 5, 6, 9
N_SEMS = 11


def ring(step):
    return min(step, 4 - step)


ROW_STEPS = sorted(
    [(a, b) for a in range(4) for b in range(4) if a or b], key=lambda s: -ring(s[0]) - ring(s[1])
)
COL_STEPS = sorted([(a, b) for a in range(4) for b in range(2) if a or b], key=lambda s: -ring(s[0]))


def iota(shape, dim):
    return lax.broadcasted_iota(jnp.int32, shape, dim)


def hot(condition):
    return jnp.where(condition, 1.0, 0.0).astype(BF16)


def dot(a, b):
    return jnp.dot(a, b, preferred_element_type=F32)


def to_column(row, size):
    shape = (size, row.shape[1])
    return jnp.sum(jnp.where(iota(shape, 0) == iota(shape, 1), row, 0.0), axis=1, keepdims=True)


def unit_rows(values):
    return values / jnp.sqrt(jnp.mean(values * values, axis=1, keepdims=True) + EPSILON)


def kernel(
    frames, counts_in, idents_in, seeds_in, query_in, emb_weight, plda_in, out,
    counts, idents, seeds, query, plda, frame_buf, weight_buf, segments, seg_totals, projected_segs,
    same_slot, place_hot, early_send, early_in, packed, inbox, row_units, col_units, metas, meta_own,
    affinity, parts, part_send, part_in, tot_send, tot_in, labels_buf,
    small_sem, frame_sem, weight_sem, send, recv,
):
    r = lax.axis_index("row")
    c = lax.axis_index("col")
    row_peers = [
        (lax.rem(r // 4 + a, 4) * 4 + lax.rem(lax.rem(r, 4) + b, 4), c) for a, b in ROW_STEPS
    ]
    col_peers = [
        (r, lax.rem(c // 2 + a, 4) * 2 + lax.rem(lax.rem(c, 2) + b, 2)) for a, b in COL_STEPS
    ]

    def wait_bytes(ref, sem):
        pltpu.make_async_copy(ref, ref, sem).wait()

    def post(src, dst, slot, peer):
        pltpu.make_async_remote_copy(
            src, dst, send.at[slot], recv.at[slot], device_id=peer, device_id_type=MESH
        ).start()

    def frame_copy(w):
        return pltpu.make_async_copy(
            frames.at[pl.ds(w * WIN, WIN)], frame_buf.at[w], frame_sem.at[w]
        )

    small_copies = [
        pltpu.make_async_copy(src, dst, small_sem.at[k])
        for k, (src, dst) in enumerate(
            (
                (counts_in, counts), (idents_in, idents), (query_in, query), (seeds_in, seeds),
                (plda_in, plda),
            )
        )
    ]
    for copy in small_copies[:4]:
        copy.start()
    for w in range(WINDOWS):
        frame_copy(w).start()
    weight_copy = pltpu.make_async_copy(emb_weight, weight_buf, weight_sem)
    weight_copy.start()
    small_copies[4].start()
    barrier = pltpu.get_barrier_semaphore()
    for peer in row_peers + col_peers:
        pl.semaphore_signal(barrier, inc=1, device_id=peer, device_id_type=MESH)
    for copy in small_copies[:4]:
        copy.wait()

    live_row = counts[...].astype(F32)
    square = (SLOTS, SLOTS)
    ends = jnp.sum(
        jnp.where(iota(square, 1) <= iota(square, 0), live_row, 0.0), axis=1, keepdims=True
    )
    count_col = to_column(live_row, SLOTS)
    ident_row = idents[...]
    dest_row = jnp.where(counts[...] > 0, ident_row // (HOME * COLS), ROWS).astype(F32)
    dest_col = to_column(dest_row, SLOTS)
    place_col = to_column((ident_row % HOME).astype(F32), SLOTS)
    rank_col = jnp.sum(
        jnp.where((dest_col == dest_row) & (iota(square, 1) < iota(square, 0)), 1.0, 0.0),
        axis=1, keepdims=True,
    )
    wide = (SLOTS, SEGS)
    before = jnp.where(ends <= (iota(wide, 1) // SEG * WIN).astype(F32), 1.0, 0.0)
    target_row = jnp.sum(before, axis=0, keepdims=True) + (iota((1, SEGS), 1) % SEG).astype(F32)
    same_slot[...] = hot(to_column(target_row, SEGS) == target_row)
    spot = jnp.where(target_row == iota(wide, 0).astype(F32), dest_col * 8.0 + rank_col + 1.0, 0.0)
    spot_row = jnp.sum(spot, axis=0, keepdims=True) - 1.0
    letter_row = iota((SEGS, SEGS), 0)
    place_hot[...] = hot(spot_row == (letter_row // 8 * 8 + letter_row % 4).astype(F32))
    lane = iota((SLOTS, 128), 1)
    mine = (lane // 8 == r) & ((lane % 4).astype(F32) == rank_col)
    high_col = jnp.floor(count_col * (1.0 / 256.0))
    notes = jnp.concatenate(
        [jnp.where(mine, v, 0.0) for v in (place_col + 1.0, high_col, count_col - 256.0 * high_col)],
        axis=1,
    ).astype(BF16)
    notes = dot(hot(dest_row == iota((ROWS, SLOTS), 0).astype(F32)), notes)
    for k in range(ROWS):
        early_send[k] = jnp.concatenate(
            [notes[k : k + 1, :128], 256.0 * notes[k : k + 1, 128:256] + notes[k : k + 1, 256:]],
            axis=1,
        )

    query_t = query[...]

    def score(w):
        frame_copy(w).wait()
        return lax.dot_general(query_t, frame_buf[w], NT, preferred_element_type=F32)

    def pool(w, scores):
        energy = jnp.exp(GAIN * jnp.tanh(scores))
        first = (w * WIN).astype(F32)
        index = first + iota((1, WIN), 1).astype(F32)
        passed = jnp.where((ends <= index) & (ends > first), 1.0, 0.0)
        rel = jnp.sum(passed, axis=0, keepdims=True)
        mask = rel == iota((SEG, WIN), 0).astype(F32)
        rows = jnp.concatenate(
            [jnp.where(mask, energy[h : h + 1, :], 0.0) for h in range(HEADS)], axis=0
        )
        sums = jnp.sum(rows, axis=1, keepdims=True)
        totals = jnp.zeros((SEG, 128), F32)
        for h in range(HEADS):
            totals = jnp.where(iota((SEG, 128), 1) == h, sums[h * SEG : (h + 1) * SEG], totals)
        seg_totals[pl.ds(pl.multiple_of(w * SEG, SEG), SEG), :] = totals
        pooled = dot(rows.astype(BF16), frame_buf[w])
        for h in range(HEADS):
            segments[h, pl.ds(pl.multiple_of(w * SEG, SEG), SEG), :] = pooled[
                h * SEG : (h + 1) * SEG
            ].astype(BF16)

    def two_windows(t, carry):
        first = score(2 * t)
        second = score(2 * t + 1)
        pool(2 * t, first)
        pool(2 * t + 1, second)
        return carry

    lax.fori_loop(0, WINDOWS // 4, two_windows, 0)
    pl.semaphore_wait(barrier, ROWS + COLS - 2)
    for peer in row_peers:
        post(early_send.at[peer[0]], early_in.at[r], EARLY, peer)
    early_in[r] = early_send[r]
    lax.fori_loop(WINDOWS // 4, WINDOWS // 2, two_windows, 0)

    high = seg_totals[...].astype(BF16)
    low = (seg_totals[...] - high.astype(F32)).astype(BF16)
    slot_totals = dot(same_slot[...], high) + dot(same_slot[...], low)
    inverse = jnp.where(slot_totals > 0.0, 1.0 / slot_totals, 0.0)
    weight_copy.wait()
    for h in range(HEADS):
        through = dot(segments[h], weight_buf[h * D : (h + 1) * D, :])
        projected_segs[h * SEGS : (h + 1) * SEGS, :] = (through * inverse[:, h : h + 1]).astype(BF16)
    letters = dot(jnp.concatenate([place_hot[...]] * HEADS, axis=1), projected_segs[...])
    packed[...] = jnp.where(iota((128, 128), 0) % 8 < 4, letters[:, :128], letters[:, 128:])
    for peer in row_peers:
        post(
            packed.at[pl.ds(pl.multiple_of(peer[0] * 8, 8), 8)],
            inbox.at[pl.ds(pl.multiple_of(r * 8, 8), 8)], PACK, peer,
        )
    own = pl.multiple_of(r * 8, 8)
    inbox[pl.ds(own, 8), :] = packed[pl.ds(own, 8), :]

    wait_bytes(early_in.at[pl.ds(0, ROWS - 1)], recv.at[EARLY])
    note = early_in[0]
    for k in range(1, ROWS):
        note = note + early_in[k]
    sub = iota((2 * HOME, 128), 0)
    lane = iota((2 * HOME, 128), 1)
    found = (note[:, :128] == (sub % HOME + 1).astype(F32)) & (lane // 4 % 2 == sub // HOME)
    pick = hot(found)
    home_len = jnp.sum(jnp.where(found, note[:, 128:], 0.0)[:HOME], axis=1, keepdims=True)
    seed_col = to_column(jnp.minimum(seeds[...], K).astype(F32), HOME)
    seed_hot = jnp.where(seed_col == iota((HOME, K), 1).astype(F32), 1.0, 0.0)
    home_high = jnp.floor(home_len * (1.0 / 256.0))
    group = iota((HOME, 128), 1) // HOME
    values = jnp.where(
        group == 0, home_high, jnp.where(group == 1, home_len - 256.0 * home_high, seed_col)
    )
    diagonal = iota((HOME, 128), 0) == iota((HOME, 128), 1) % HOME
    meta_own[0] = jnp.sum(jnp.where(diagonal, values, 0.0), axis=0, keepdims=True)
    metas[r] = meta_own[0]
    for peer in row_peers:
        post(meta_own.at[0], metas.at[r], META, peer)
    small_copies[4].wait()

    row_own = pl.multiple_of(c * HOME, HOME)
    col_own = pl.multiple_of(r * HOME, HOME)
    wait_bytes(inbox.at[pl.ds(0, (ROWS - 1) * 8)], recv.at[PACK])
    halves = dot(pick, inbox[...].astype(BF16))
    home_embed = jnp.concatenate([halves[:HOME], halves[HOME:]], axis=1)
    row_units[pl.ds(row_own, HOME), :] = unit_rows(home_embed).astype(BF16)
    projected = dot(home_embed.astype(BF16), plda[...])
    col_units[pl.ds(col_own, HOME), :] = unit_rows(projected).astype(BF16)
    for peer in row_peers:
        post(
            col_units.at[pl.ds(col_own, HOME)], col_units.at[pl.ds(col_own, HOME)], COLU, peer
        )
    for peer in col_peers:
        post(
            row_units.at[pl.ds(row_own, HOME)], row_units.at[pl.ds(row_own, HOME)], ROWU, peer
        )

    wait_bytes(metas.at[pl.ds(0, ROWS - 1)], recv.at[META])
    shape = (128, ROWS * HOME)
    spread_lane = iota(shape, 1) % HOME
    spread_sub = iota(shape, 0)
    take_len = jnp.where(spread_sub == spread_lane, 256.0, 0.0) + jnp.where(
        spread_sub == spread_lane + HOME, 1.0, 0.0
    )
    take_seed = jnp.where(spread_sub == spread_lane + 2 * HOME, 1.0, 0.0)
    meta_rows = jnp.concatenate([metas[k] for k in range(ROWS)], axis=0).astype(BF16)
    on_row = iota((ROWS, ROWS * HOME), 0) == iota((ROWS, ROWS * HOME), 1) // HOME

    def column_row(take):
        full = dot(meta_rows, take.astype(BF16))
        return jnp.sum(jnp.where(on_row, full, 0.0), axis=0, keepdims=True)

    len_row = column_row(take_len) * (1.0 / FPU)
    seeds_row = column_row(take_seed)
    labels_buf[0] = (
        jnp.where(seeds_row == iota((K, ROWS * HOME), 0).astype(F32), 1.0, 0.0).T.astype(BF16)
    )

    wait_bytes(row_units.at[pl.ds(0, (COLS - 1) * HOME)], recv.at[ROWU])
    wait_bytes(col_units.at[pl.ds(0, (ROWS - 1) * HOME)], recv.at[COLU])
    cosine = lax.dot_general(row_units[...], col_units[...], NT, preferred_element_type=F32)
    affinity[...] = (len_row * jnp.exp(cosine * (BETA / E))).astype(BF16)

    totals = None
    for step in range(ITERS):
        if step > 0:
            wait_bytes(labels_buf.at[step, pl.ds(0, (ROWS - 1) * HOME)], recv.at[LABS + step - 1])
        part = dot(affinity[...], labels_buf[step])
        part_send[step] = part.astype(BF16)
        for k, peer in enumerate(col_peers):
            post(
                part_send.at[step, pl.ds(pl.multiple_of(peer[1] * HOME, HOME), HOME)],
                part_in.at[step, k], SUMS + step, peer,
            )
        parts[...] = part
        if step == 0:
            tot_send[0] = lax.dot_general(
                jnp.ones((8, ROWS * HOME), BF16), affinity[...], NT, preferred_element_type=F32
            )[0:1]
            for k, peer in enumerate(col_peers):
                post(tot_send.at[0], tot_in.at[k], TOTS, peer)
            wait_bytes(tot_in, recv.at[TOTS])
            row_totals = tot_send[0]
            for k in range(COLS - 1):
                row_totals = row_totals + tot_in[k]
            here = iota((HOME, COLS * HOME), 1) == iota((HOME, COLS * HOME), 0) + c * HOME
            totals = jnp.sum(jnp.where(here, row_totals, 0.0), axis=1, keepdims=True)
        wait_bytes(part_in.at[step], recv.at[SUMS + step])
        spread = parts[pl.ds(row_own, HOME), :]
        for k in range(COLS - 1):
            spread = spread + part_in[step, k].astype(F32)
        labels = ALPHA * spread / totals + (1.0 - ALPHA) * seed_hot
        if step < ITERS - 1:
            labels_buf[step + 1, pl.ds(col_own, HOME), :] = labels.astype(BF16)
            for peer in row_peers:
                post(
                    labels_buf.at[step + 1, pl.ds(col_own, HOME)],
                    labels_buf.at[step + 1, pl.ds(col_own, HOME)], LABS + step, peer,
                )
        else:
            out[...] = jnp.log(1.0 + K * labels)

    wait_bytes(early_in.at[pl.ds(0, ROWS - 1)], send.at[EARLY])
    wait_bytes(inbox.at[pl.ds(0, (ROWS - 1) * 8)], send.at[PACK])
    wait_bytes(row_units.at[pl.ds(0, (COLS - 1) * HOME)], send.at[ROWU])
    wait_bytes(col_units.at[pl.ds(0, (ROWS - 1) * HOME)], send.at[COLU])
    wait_bytes(metas.at[pl.ds(0, ROWS - 1)], send.at[META])
    wait_bytes(tot_in, send.at[TOTS])
    for step in range(ITERS):
        wait_bytes(part_in.at[step], send.at[SUMS + step])
    for step in range(ITERS - 1):
        wait_bytes(labels_buf.at[step + 1, pl.ds(0, (ROWS - 1) * HOME)], send.at[LABS + step])


def on_device(frames, frame_counts, slot_ids, seed_labels, attn_query, emb_weight, plda_weight):
    vmem = pl.BlockSpec(memory_space=pltpu.VMEM)
    hbm = pl.BlockSpec(memory_space=pl.ANY)
    return pl.pallas_call(
        kernel,
        name="speaker_linking",
        out_shape=jax.ShapeDtypeStruct((HOME, K), F32),
        in_specs=[hbm] * 7,
        out_specs=vmem,
        scratch_shapes=[
            pltpu.VMEM((1, SLOTS), jnp.int32),
            pltpu.VMEM((1, SLOTS), jnp.int32),
            pltpu.VMEM((1, HOME), jnp.int32),
            pltpu.VMEM((HEADS, D), BF16),
            pltpu.VMEM((E, E), BF16),
            pltpu.VMEM((WINDOWS, WIN, D), BF16),
            pltpu.VMEM((HEADS * D, E), BF16),
            pltpu.VMEM((HEADS, SEGS, D), BF16),
            pltpu.VMEM((SEGS, 128), F32),
            pltpu.VMEM((HEADS * SEGS, E), BF16),
            pltpu.VMEM((SEGS, SEGS), BF16),
            pltpu.VMEM((SEGS, SEGS), BF16),
            pltpu.VMEM((ROWS, 1, 256), F32),
            pltpu.VMEM((ROWS, 1, 256), F32),
            pltpu.VMEM((ROWS * 8, 128), F32),
            pltpu.VMEM((ROWS * 8, 128), F32),
            pltpu.VMEM((COLS * HOME, E), BF16),
            pltpu.VMEM((ROWS * HOME, E), BF16),
            pltpu.VMEM((ROWS, 1, 128), F32),
            pltpu.VMEM((1, 1, 128), F32),
            pltpu.VMEM((COLS * HOME, ROWS * HOME), BF16),
            pltpu.VMEM((COLS * HOME, K), F32),
            pltpu.VMEM((ITERS, COLS * HOME, K), BF16),
            pltpu.VMEM((ITERS, COLS - 1, HOME, K), BF16),
            pltpu.VMEM((1, 1, COLS * HOME), F32),
            pltpu.VMEM((COLS - 1, 1, COLS * HOME), F32),
            pltpu.VMEM((ITERS, ROWS * HOME, K), BF16),
            pltpu.SemaphoreType.DMA((5,)),
            pltpu.SemaphoreType.DMA((WINDOWS,)),
            pltpu.SemaphoreType.DMA,
            pltpu.SemaphoreType.DMA((N_SEMS,)),
            pltpu.SemaphoreType.DMA((N_SEMS,)),
        ],
        compiler_params=pltpu.CompilerParams(
            collective_id=0, has_side_effects=True, vmem_limit_bytes=60 * 1024 * 1024
        ),
    )(
        frames, frame_counts, slot_ids, seed_labels.reshape(1, HOME), attn_query.T, emb_weight,
        plda_weight,
    )


def solution(mesh):
    return jax.shard_map(
        on_device,
        mesh=mesh,
        in_specs=(
            P(("row", "col"), None),
            P(("row", "col"), None),
            P(("row", "col"), None),
            P(("row", "col")),
            P(),
            P(),
            P(),
        ),
        out_specs=P(("row", "col"), None),
        check_vma=False,
    )
```

time: 61.3 us -> 56.1 us (0.915)
  local copies, waits for them, and re-layouts: 6.55 us -> 1.38 us
    unnamed x12 -> x1, local copies, waits for them, and re-layouts: 6.55 us -> 1.38 us
where the time goes in v2:
time: 56.1 us; the launch traced here: 56 us
  Pallas kernels  54.6 us (97%)
  local copies, waits for them, and re-layouts  1.38 us (2%)
    pallas_call x1, Pallas kernels, on_device(): pl.pallas_call(kernel, name='speaker_linking', out_shape=jax.ShapeDtypeSt...  54.6 us
    unnamed x1, local copies, waits for them, and re-layouts  1.38 us

profile of v2, /device:TPU:1, one launch (start us, length us, event | category | flops | bytes accessed | tf_op | source)
XLA Modules:
  0.0 56.0 jit_solution(7603782926871245008)
XLA Ops:
  0.0 54.6 %speaker_linking.1 = f32[32,256]{1,0:T(8,128)} custom-call(bf16[8192,1024]{1,0:T(8,128)(2,1)} %frames.1, s32[1,64]{1,0:T(1,128)} %counts_in.1, s32[1,64]{1,0:T(1,128)} %idents_in.1, s32[1,32]{1,0:T(1,128)} %bitcast.3, bf16[8,1024]{1,0:T(8,128)(2,1)} %bitcast.2, bf16[8192,256]{1,0:T(8,128)(2,1)} %emb_weight.1, bf16[256,256]{1,0:T(8,128)(2,1)} %plda_in.1), custom_call_target="tpu_custom_call" | custom-call | tf_op jit(solution)/shard_map/speaker_linking/pallas_call | solution.py:335
  54.6 1.4 %copy.9 = f32[32,256]{1,0:T(8,128)} copy(f32[32,256]{1,0:T(8,128)} %speaker_linking.1) | data formatting | bytes 65536

commit v3 on v2

--- a/solution.py
+++ b/solution.py
@@ -106,16 +106,18 @@
     ]
     for copy in small_copies[:4]:
         copy.start()
-    for w in range(WINDOWS):
+    for w in range(2):
         frame_copy(w).start()
-    weight_copy = pltpu.make_async_copy(emb_weight, weight_buf, weight_sem)
-    weight_copy.start()
-    small_copies[4].start()
     barrier = pltpu.get_barrier_semaphore()
     for peer in row_peers + col_peers:
         pl.semaphore_signal(barrier, inc=1, device_id=peer, device_id_type=MESH)
     for copy in small_copies[:4]:
         copy.wait()
+    for w in range(2, WINDOWS):
+        frame_copy(w).start()
+    weight_copy = pltpu.make_async_copy(emb_weight, weight_buf, weight_sem)
+    weight_copy.start()
+    small_copies[4].start()
 
     live_row = counts[...].astype(F32)
     square = (SLOTS, SLOTS)

time: 56.1 us -> 53.1 us (0.947)
  Pallas kernels: 54.6 us -> 51.6 us
    pallas_call x1, Pallas kernels: 54.6 us -> 51.6 us  [on_device(): pl.pallas_call(kernel, name='speaker_linking', out_shape=jax.ShapeDtypeSt...]
where the time goes in v3:
time: 53.1 us; the launch traced here: 52.9 us
  Pallas kernels  51.6 us (97%)
  local copies, waits for them, and re-layouts  1.38 us (3%)
    pallas_call x1, Pallas kernels, on_device(): pl.pallas_call(kernel, name='speaker_linking', out_shape=jax.ShapeDtypeSt...  51.6 us
    unnamed x1, local copies, waits for them, and re-layouts  1.38 us

profile of v3, /device:TPU:1, one launch (start us, length us, event | category | flops | bytes accessed | tf_op | source)
XLA Modules:
  0.0 52.9 jit_solution(1610025487852516983)
XLA Ops:
  0.0 51.6 %speaker_linking.1 = f32[32,256]{1,0:T(8,128)} custom-call(bf16[8192,1024]{1,0:T(8,128)(2,1)} %frames.1, s32[1,64]{1,0:T(1,128)} %counts_in.1, s32[1,64]{1,0:T(1,128)} %idents_in.1, s32[1,32]{1,0:T(1,128)} %bitcast.3, bf16[8,1024]{1,0:T(8,128)(2,1)} %bitcast.2, bf16[8192,256]{1,0:T(8,128)(2,1)} %emb_weight.1, bf16[256,256]{1,0:T(8,128)(2,1)} %plda_in.1), custom_call_target="tpu_custom_call" | custom-call | tf_op jit(solution)/shard_map/speaker_linking/pallas_call | solution.py:337
  51.6 1.4 %copy.9 = f32[32,256]{1,0:T(8,128)} copy(f32[32,256]{1,0:T(8,128)} %speaker_linking.1) | data formatting | bytes 65536

commit v4 on v3

--- a/solution.py
+++ b/solution.py
@@ -23,6 +23,7 @@
 SEG = 16
 SEGS = WINDOWS * SEG
 ITERS = 3
+HALF = 128
 
 GAIN = 4.0
 BETA = 8.0
@@ -31,8 +32,8 @@
 
 NT = (((1,), (1,)), ((), ()))
 
-EARLY, PACK, ROWU, COLU, META, TOTS, SUMS, LABS = 0, 1, 2, 3, 4, 5, 6, 9
-N_SEMS = 11
+EARLY, PACK, ROWU, COLU, META, TOTS, SUMS, LABS = 0, 1, 2, 3, 4, 5, 6, 12
+N_SEMS = 16
 
 
 def ring(step):
@@ -271,9 +272,9 @@
 
     len_row = column_row(take_len) * (1.0 / FPU)
     seeds_row = column_row(take_seed)
-    labels_buf[0] = (
-        jnp.where(seeds_row == iota((K, ROWS * HOME), 0).astype(F32), 1.0, 0.0).T.astype(BF16)
-    )
+    start = jnp.where(seeds_row == iota((K, ROWS * HOME), 0).astype(F32), 1.0, 0.0).T.astype(BF16)
+    for half in range(2):
+        labels_buf[0, half] = start[:, half * HALF : (half + 1) * HALF]
 
     wait_bytes(row_units.at[pl.ds(0, (COLS - 1) * HOME)], recv.at[ROWU])
     wait_bytes(col_units.at[pl.ds(0, (ROWS - 1) * HOME)], recv.at[COLU])
@@ -282,16 +283,20 @@
 
     totals = None
     for step in range(ITERS):
-        if step > 0:
-            wait_bytes(labels_buf.at[step, pl.ds(0, (ROWS - 1) * HOME)], recv.at[LABS + step - 1])
-        part = dot(affinity[...], labels_buf[step])
-        part_send[step] = part.astype(BF16)
-        for k, peer in enumerate(col_peers):
-            post(
-                part_send.at[step, pl.ds(pl.multiple_of(peer[1] * HOME, HOME), HOME)],
-                part_in.at[step, k], SUMS + step, peer,
-            )
-        parts[...] = part
+        for half in range(2):
+            if step > 0:
+                wait_bytes(
+                    labels_buf.at[step, half, pl.ds(0, (ROWS - 1) * HOME)],
+                    recv.at[LABS + 2 * step - 2 + half],
+                )
+            part = dot(affinity[...], labels_buf[step, half])
+            part_send[step, half] = part.astype(BF16)
+            for k, peer in enumerate(col_peers):
+                post(
+                    part_send.at[step, half, pl.ds(pl.multiple_of(peer[1] * HOME, HOME), HOME)],
+                    part_in.at[step, half, k], SUMS + 2 * step + half, peer,
+                )
+            parts[half] = part
         if step == 0:
             tot_send[0] = lax.dot_general(
                 jnp.ones((8, ROWS * HOME), BF16), affinity[...], NT, preferred_element_type=F32
@@ -304,20 +309,24 @@
                 row_totals = row_totals + tot_in[k]
             here = iota((HOME, COLS * HOME), 1) == iota((HOME, COLS * HOME), 0) + c * HOME
             totals = jnp.sum(jnp.where(here, row_totals, 0.0), axis=1, keepdims=True)
-        wait_bytes(part_in.at[step], recv.at[SUMS + step])
-        spread = parts[pl.ds(row_own, HOME), :]
-        for k in range(COLS - 1):
-            spread = spread + part_in[step, k].astype(F32)
-        labels = ALPHA * spread / totals + (1.0 - ALPHA) * seed_hot
-        if step < ITERS - 1:
-            labels_buf[step + 1, pl.ds(col_own, HOME), :] = labels.astype(BF16)
-            for peer in row_peers:
-                post(
-                    labels_buf.at[step + 1, pl.ds(col_own, HOME)],
-                    labels_buf.at[step + 1, pl.ds(col_own, HOME)], LABS + step, peer,
-                )
-        else:
-            out[...] = jnp.log(1.0 + K * labels)
+        for half in range(2):
+            wait_bytes(part_in.at[step, half], recv.at[SUMS + 2 * step + half])
+            spread = parts[half, pl.ds(row_own, HOME), :]
+            for k in range(COLS - 1):
+                spread = spread + part_in[step, half, k].astype(F32)
+            labels = ALPHA * spread / totals + (1.0 - ALPHA) * seed_hot[
+                :, half * HALF : (half + 1) * HALF
+            ]
+            if step < ITERS - 1:
+                labels_buf[step + 1, half, pl.ds(col_own, HOME), :] = labels.astype(BF16)
+                for peer in row_peers:
+                    post(
+                        labels_buf.at[step + 1, half, pl.ds(col_own, HOME)],
+                        labels_buf.at[step + 1, half, pl.ds(col_own, HOME)],
+                        LABS + 2 * step + half, peer,
+                    )
+            else:
+                out[:, half * HALF : (half + 1) * HALF] = jnp.log(1.0 + K * labels)
 
     wait_bytes(early_in.at[pl.ds(0, ROWS - 1)], send.at[EARLY])
     wait_bytes(inbox.at[pl.ds(0, (ROWS - 1) * 8)], send.at[PACK])
@@ -326,9 +335,14 @@
     wait_bytes(metas.at[pl.ds(0, ROWS - 1)], send.at[META])
     wait_bytes(tot_in, send.at[TOTS])
     for step in range(ITERS):
-        wait_bytes(part_in.at[step], send.at[SUMS + step])
+        for half in range(2):
+            wait_bytes(part_in.at[step, half], send.at[SUMS + 2 * step + half])
     for step in range(ITERS - 1):
-        wait_bytes(labels_buf.at[step + 1, pl.ds(0, (ROWS - 1) * HOME)], send.at[LABS + step])
+        for half in range(2):
+            wait_bytes(
+                labels_buf.at[step + 1, half, pl.ds(0, (ROWS - 1) * HOME)],
+                send.at[LABS + 2 * step + half],
+            )
 
 
 def on_device(frames, frame_counts, slot_ids, seed_labels, attn_query, emb_weight, plda_weight):
@@ -362,12 +376,12 @@
             pltpu.VMEM((ROWS, 1, 128), F32),
             pltpu.VMEM((1, 1, 128), F32),
             pltpu.VMEM((COLS * HOME, ROWS * HOME), BF16),
-            pltpu.VMEM((COLS * HOME, K), F32),
-            pltpu.VMEM((ITERS, COLS * HOME, K), BF16),
-            pltpu.VMEM((ITERS, COLS - 1, HOME, K), BF16),
+            pltpu.VMEM((2, COLS * HOME, HALF), F32),
+            pltpu.VMEM((ITERS, 2, COLS * HOME, HALF), BF16),
+            pltpu.VMEM((ITERS, 2, COLS - 1, HOME, HALF), BF16),
             pltpu.VMEM((1, 1, COLS * HOME), F32),
             pltpu.VMEM((COLS - 1, 1, COLS * HOME), F32),
-            pltpu.VMEM((ITERS, ROWS * HOME, K), BF16),
+            pltpu.VMEM((ITERS, 2, ROWS * HOME, HALF), BF16),
             pltpu.SemaphoreType.DMA((5,)),
             pltpu.SemaphoreType.DMA((WINDOWS,)),
             pltpu.SemaphoreType.DMA,

time: 53.1 us -> 52.3 us (0.985)
  Pallas kernels: 51.6 us -> 50.8 us
    pallas_call x1, Pallas kernels: 51.6 us -> 50.8 us  [on_device(): pl.pallas_call(kernel, name='speaker_linking', out_shape=jax.ShapeDtypeSt...]
where the time goes in v4:
time: 52.3 us; the launch traced here: 52.1 us
  Pallas kernels  50.8 us (97%)
  local copies, waits for them, and re-layouts  1.38 us (3%)
    pallas_call x1, Pallas kernels, on_device(): pl.pallas_call(kernel, name='speaker_linking', out_shape=jax.ShapeDtypeSt...  50.8 us
    unnamed x1, local copies, waits for them, and re-layouts  1.38 us

profile of v4, /device:TPU:1, one launch (start us, length us, event | category | flops | bytes accessed | tf_op | source)
XLA Modules:
  0.0 52.1 jit_solution(8718043575310667761)
XLA Ops:
  0.0 50.8 %speaker_linking.1 = f32[32,256]{1,0:T(8,128)} custom-call(bf16[8192,1024]{1,0:T(8,128)(2,1)} %frames.1, s32[1,64]{1,0:T(1,128)} %counts_in.1, s32[1,64]{1,0:T(1,128)} %idents_in.1, s32[1,32]{1,0:T(1,128)} %bitcast.3, bf16[8,1024]{1,0:T(8,128)(2,1)} %bitcast.2, bf16[8192,256]{1,0:T(8,128)(2,1)} %emb_weight.1, bf16[256,256]{1,0:T(8,128)(2,1)} %plda_in.1), custom_call_target="tpu_custom_call" | custom-call | tf_op jit(solution)/shard_map/speaker_linking/pallas_call | solution.py:351
  50.8 1.4 %copy.9 = f32[32,256]{1,0:T(8,128)} copy(f32[32,256]{1,0:T(8,128)} %speaker_linking.1) | data formatting | bytes 65536

commit v5 on v4

--- a/solution.py
+++ b/solution.py
@@ -351,7 +351,7 @@
     return pl.pallas_call(
         kernel,
         name="speaker_linking",
-        out_shape=jax.ShapeDtypeStruct((HOME, K), F32),
+        out_shape=pltpu.VMEM((HOME, K), F32),
         in_specs=[hbm] * 7,
         out_specs=vmem,
         scratch_shapes=[

time: 52.3 us -> 50.9 us (0.973)
  local copies, waits for them, and re-layouts: 1.38 us -> 0.62 us
  Pallas kernels: 50.8 us -> 50.1 us
    unnamed x1, local copies, waits for them, and re-layouts: 1.38 us -> 0.62 us
    pallas_call x1, Pallas kernels: 50.8 us -> 50.1 us  [on_device(): pl.pallas_call(kernel, name='speaker_linking', out_shape=pltpu.VMEM((HOME...]
where the time goes in v5:
time: 50.9 us; the launch traced here: 50.8 us
  Pallas kernels  50.1 us (98%)
  local copies, waits for them, and re-layouts  0.62 us (1%)
    pallas_call x1, Pallas kernels, on_device(): pl.pallas_call(kernel, name='speaker_linking', out_shape=pltpu.VMEM((HOME...  50.1 us

profile of v5, /device:TPU:1, one launch (start us, length us, event | category | flops | bytes accessed | tf_op | source)
XLA Modules:
  0.0 50.8 jit_solution(17617105159023554432)
XLA Ops:
  0.0 50.1 %speaker_linking.1 = f32[32,256]{1,0:T(8,128)S(1)} custom-call(bf16[8192,1024]{1,0:T(8,128)(2,1)} %frames.1, s32[1,64]{1,0:T(1,128)} %counts_in.1, s32[1,64]{1,0:T(1,128)} %idents_in.1, s32[1,32]{1,0:T(1,128)} %bitcast.3, bf16[8,1024]{1,0:T(8,128)(2,1)} %bitcast.2, bf16[8192,256]{1,0:T(8,128)(2,1)} %emb_weight.1, bf16[256,256]{1,0:T(8,128)(2,1)} %plda_in.1), custom_call_target="tpu_custom_call" | custom-call | tf_op jit(solution)/shard_map/speaker_linking/pallas_call | solution.py:351
  50.2 0.6 %copy.9 = f32[32,256]{1,0:T(8,128)} copy(f32[32,256]{1,0:T(8,128)S(1)} %speaker_linking.1) | data formatting | bytes 65536
